TPU v7x, 32 devices: a whole 2x2x4 slice. The times are simulated.
32 devices in a mesh: wide: 8 (over y, x, core), narrow: 4 (over z).
Axes of the slice: x: 2, y: 2, z: 4, core: 2. Of those that a mesh axis runs over, the one named last changes fastest.
Arguments:
- charges: float32 [2, 64, 8192], P(None, None, ('wide', 'narrow')), may hold values from -6 to 6
- projection: float32 [64, 64], replicated, may hold values from -0.75 to 0.75
- green_hat: float32 [2, 256, 64, 512], P(None, ('wide', 'narrow')), may hold values from -6 to 6
- near_table: float32 [27, 2, 64, 64], replicated, may hold values from -0.109375 to 0.109375
- block_site: int32 [8192], P(('wide', 'narrow')), may hold values from 0 to 511, as said below
- block_count: int32 [32], P(('wide', 'narrow')), may hold values from 128 to 256, as said below
- near_source: int32 [27, 8192], P(None, ('wide', 'narrow')), may hold values from 0 to 2303
Outputs:
- result: float32 [2, 64, 8192], P(None, None, ('wide', 'narrow'))
Inputs may be any that keep to these rules, and one draw needn't show every extreme that they name: `block_count`: slots at or beyond a device's count hold no block; at least one device has all 256 slots occupied. `block_site`: distinct among the slots of one device.
All inputs are finite; a program needn't handle non-finite values.
Results may differ from a plain program's by a relative error of at most 0.0003.
Values sent between devices are 32-bit elements; how exact they have to be, the bound alone decides.
A program may use at most 128 MiB of HBM per device.

v0:
```python
import functools

import jax
import jax.numpy as jnp
import ml_dtypes
import numpy as np
from jax import lax
from jax.experimental import pallas as pl
from jax.experimental.pallas import tpu as pltpu
from jax.sharding import PartitionSpec as P

PX = 4
PY = 64
PZ = 128
SPAN_Y = PY // 4
SPAN_Z = PZ // 4
ROW = 2 * PY
WIDTH = PX * ROW
VMEM_LIMIT = 48 * 1024 * 1024
F32 = jnp.float32
BF16 = jnp.bfloat16


def halves(table):
    high = table.astype(np.float32).astype(ml_dtypes.bfloat16)
    low = (table - high.astype(np.float64)).astype(np.float32).astype(ml_dtypes.bfloat16)
    return high, low


def waves(left, right, length):
    angles = 2.0 * np.pi * (np.outer(left, right) % length) / length
    return np.cos(angles), np.sin(angles)


@functools.lru_cache(maxsize=None)
def constant_tables(wide_count, narrow_count):
    whole_x = 2 * PX * wide_count
    whole_y = 2 * PY * narrow_count
    whole_z = 2 * PZ
    ez, ex, part, ey, _ = np.unravel_index(
        np.arange(4 * WIDTH), (4, PX, 2, 4, SPAN_Y)
    )
    owner = part * 64 + 16 * ex + 4 * ey + ez
    spread = (np.arange(128)[:, None] == owner[None, :]).astype(ml_dtypes.bfloat16)
    depth = (4 * np.arange(SPAN_Z)[None, :] + np.arange(4)[:, None]).reshape(-1)
    cos_z, sin_z = waves(np.arange(whole_z), depth, whole_z)
    forward_z = np.concatenate([cos_z, sin_z], axis=1)
    inverse_z = np.concatenate([cos_z.T, sin_z.T], axis=1) / (whole_x * whole_y * whole_z)
    line = (4 * np.arange(SPAN_Y)[None, :] + np.arange(4)[:, None]).reshape(-1)
    points = (PY * np.arange(narrow_count)[:, None] + line[None, :]).reshape(-1)
    cos_y, sin_y = waves(points, np.arange(whole_y), whole_y)
    real_rows = np.concatenate([cos_y, -sin_y], axis=1).reshape(narrow_count, 1, PY, 2 * whole_y)
    imag_rows = np.concatenate([sin_y, cos_y], axis=1).reshape(narrow_count, 1, PY, 2 * whole_y)
    forward_y = np.concatenate([real_rows, imag_rows], axis=1).reshape(-1, 2 * whole_y)
    cos_x, sin_x = waves(np.arange(whole_x), np.arange(whole_x // 2), whole_x)
    forward_x = np.block([[cos_x, sin_x], [-sin_x, cos_x]])
    packed = []
    for table in (forward_x, forward_x.T):
        high, low = halves(table)
        packed.append(np.concatenate([high, high, low], axis=1))
    return {
        "spread": spread,
        "gather": np.ascontiguousarray(spread.T),
        "forward_z": halves(forward_z),
        "inverse_z": halves(inverse_z),
        "forward_y": halves(forward_y),
        "inverse_y": halves(np.ascontiguousarray(forward_y.T)),
        "forward_x": packed[0],
        "inverse_x": packed[1],
    }


def split(values):
    high = values.astype(BF16)
    return high, (values - high.astype(F32)).astype(BF16)


def dot(left, right, dims=((1,), (0,))):
    return lax.dot_general(left, right, (dims, ((), ())), preferred_element_type=F32)


def dot3(left, right, dims=((1,), (0,))):
    lh, ll = left
    rh, rl = right
    return dot(lh, rh, dims) + (dot(ll, rh, dims) + dot(lh, rl, dims))


def turned(values, sign):
    lanes = lax.broadcasted_iota(jnp.int32, (values.shape[0], ROW), 1)
    factor = jnp.where(lanes < PY, sign, -sign).astype(F32)
    pieces = [
        pltpu.roll(values[:, i * ROW : (i + 1) * ROW], PY, 1) * factor
        for i in range(values.shape[1] // ROW)
    ]
    return jnp.concatenate(pieces, axis=1)


def columns_of(row, slots):
    return jnp.broadcast_to(row.astype(F32), (128, slots)).T


def own_line(site, slots):
    line = columns_of(site // SPAN_Z, slots)
    lanes = lax.broadcasted_iota(jnp.int32, (slots, 128), 1) % SPAN_Y
    match = line == lanes.astype(F32)
    return jnp.concatenate([match.astype(F32)] * (WIDTH // 128), axis=1)


def place_kernel(count, charges, projection, site, spread, zh, zl, masked_out, send):
    slots = charges.shape[2]
    slot = lax.broadcasted_iota(jnp.int32, (1, slots), 1)
    occupied = (slot < count[0]).astype(F32)
    parts = [charges[r] * occupied for r in range(2)]
    masked_out[...] = jnp.concatenate(parts, axis=0).T
    weights = split(projection[...])
    stencil = jnp.concatenate([dot3(weights, split(p)) for p in parts], axis=0).T
    high, low = split(stencil)
    table = spread[...]
    spread_out = dot(
        jnp.concatenate([high, low], axis=1), jnp.concatenate([table, table], axis=0)
    )
    mask = own_line(site[...], slots)
    depth = lax.broadcasted_iota(jnp.int32, (SPAN_Z, slots), 0)
    picker = (depth == site[...] % SPAN_Z).astype(F32).astype(BF16)
    rows = []
    for ez in range(4):
        high, low = split(spread_out[:, ez * WIDTH : (ez + 1) * WIDTH] * mask)
        rows.append(dot(picker, high) + dot(picker, low))
    grid = jnp.concatenate(rows, axis=0)
    both = jnp.concatenate([grid, turned(grid, 1.0)], axis=0)
    freq = dot3((zh[...], zl[...]), split(both))
    planes = send.shape[1] // PX
    for ex in range(PX):
        block = freq[:, ex * ROW : (ex + 1) * ROW]
        send[:, ex * planes : (ex + 1) * planes, :] = block.reshape(send.shape[0], planes, ROW)


def plane_kernel(wide, narrow, recv, green, fyh, fyl, iyh, iyl, fx, ix, send, lines, back):
    planes = green.shape[1]
    whole_x, whole_y = green.shape[2:]
    half_x = whole_x // 2
    group = recv.shape[1]
    chunks = 2 * whole_y // 128
    values = recv[...].reshape(wide, narrow, group, ROW)
    field = jnp.concatenate(
        [values[:, n].reshape(wide * group, ROW) for n in range(narrow)], axis=1
    )
    freq = dot3(split(field), (fyh[...], fyl[...]))
    for c in range(chunks):
        lines[c] = freq[:, c * 128 : (c + 1) * 128]
    for z in range(planes):
        at = pl.ds(z, half_x, stride=planes) if planes > 1 else pl.ds(0, half_x)
        taken = [lines[c, at, :] for c in range(chunks)]
        column = jnp.concatenate(
            [
                jnp.concatenate(taken[: chunks // 2], axis=1),
                jnp.concatenate(taken[chunks // 2 :], axis=1),
            ],
            axis=0,
        )
        high, low = split(column)
        freq = dot(fx[...], jnp.concatenate([high, low, high], axis=0))
        real, imag = freq[:whole_x], freq[whole_x:]
        gr, gi = green[0, z], green[1, z]
        product = jnp.concatenate([gr * real - gi * imag, gr * imag + gi * real], axis=0)
        high, low = split(product)
        column = dot(ix[...], jnp.concatenate([high, low, high], axis=0))
        for c in range(chunks):
            part, lane = divmod(c, chunks // 2)
            back[c, at, :] = column[
                part * half_x : (part + 1) * half_x, lane * 128 : (lane + 1) * 128
            ]
    field = jnp.concatenate([back[c] for c in range(chunks)], axis=1)
    out = dot3(split(field), (iyh[...], iyl[...]))
    for n in range(narrow):
        block = out[:, n * ROW : (n + 1) * ROW].reshape(wide, group, ROW)
        for w in range(wide):
            send[w * narrow + n] = block[w]


def near_kernel(source, before, own, after, table, near, cube, picked):
    third = own.shape[0]
    cube[:third] = before[...]
    cube[third : 2 * third] = own[...]
    cube[2 * third :] = after[...]
    classes, slots = source.shape
    near[...] = jnp.zeros(near.shape, F32)

    def one_class(k, carry):
        def eight(i, inner):
            base = pl.multiple_of(i * 16, 16)
            for j in range(16):
                picked[pl.ds(base + j, 1), :] = cube[pl.ds(source[k, base + j], 1), :]
            return inner

        lax.fori_loop(0, slots // 16, eight, 0)
        real, imag = table[k, 0], table[k, 1]
        matrix = jnp.concatenate(
            [
                jnp.concatenate([real, -imag], axis=1),
                jnp.concatenate([imag, real], axis=1),
            ],
            axis=0,
        )
        near[...] += dot3(split(picked[...]), split(matrix), ((1,), (1,)))
        return carry

    lax.fori_loop(0, classes, one_class, 0)


def finish_kernel(count, recv, projection, site, gather, zh, zl, near, out):
    slots = out.shape[2]
    planes = recv.shape[1] // PX
    freq = jnp.concatenate(
        [
            recv[:, ex * planes : (ex + 1) * planes, :].reshape(recv.shape[0] * planes, ROW)
            for ex in range(PX)
        ],
        axis=1,
    )
    both = jnp.concatenate([freq, turned(freq, -1.0)], axis=0)
    grid = dot3((zh[...], zl[...]), split(both))
    mask = own_line(site[...], slots)
    depth = lax.broadcasted_iota(jnp.int32, (slots, 128), 1)
    match = columns_of(site[...] % SPAN_Z, slots) == depth.astype(F32)
    picker = match.astype(F32).astype(BF16)[:, :SPAN_Z]
    total = jnp.zeros((slots, 128), F32)
    for ez in range(4):
        high, low = split(grid[ez * SPAN_Z : (ez + 1) * SPAN_Z])
        taken = (dot(picker, high) + dot(picker, low)) * mask
        high, low = split(taken)
        table = gather[ez * WIDTH : (ez + 1) * WIDTH, :]
        total = total + (dot(high, table) + dot(low, table))
    taken = total.T
    beside = near[...].T
    weights = split(projection[...])
    slot = lax.broadcasted_iota(jnp.int32, (1, slots), 1)
    occupied = (slot < count[0]).astype(F32)
    cells = out.shape[1]
    for r in range(2):
        far = dot3(weights, split(taken[r * 64 : (r + 1) * 64]), ((0,), (0,)))
        out[r] = (far + beside[r * cells : (r + 1) * cells]) * occupied


def call(kernel, out_shape, operands, scratch=(), scalars=(), flops=0, moved=0):
    spaces = [
        pl.BlockSpec(memory_space=pltpu.SMEM if i in scalars else pltpu.VMEM)
        for i in range(len(operands))
    ]
    outs = jax.tree.map(lambda _: pl.BlockSpec(memory_space=pltpu.VMEM), out_shape)
    return pl.pallas_call(
        kernel,
        out_shape=out_shape,
        in_specs=spaces,
        out_specs=outs,
        scratch_shapes=list(scratch),
        compiler_params=pltpu.CompilerParams(vmem_limit_bytes=VMEM_LIMIT),
        cost_estimate=pl.CostEstimate(flops=flops, bytes_accessed=moved, transcendentals=0),
    )(*operands)


def shifted(array, axis, step):
    devices = lax.axis_size(axis)
    pairs = [(i, i + step) for i in range(devices) if 0 <= i + step < devices]
    return lax.ppermute(array, axis, pairs)


def per_device(charges, projection, green_hat, near_table, block_site, block_count, near_source):
    wide = lax.axis_size("wide")
    narrow = lax.axis_size("narrow")
    tables = constant_tables(wide, narrow)
    cells, slots = charges.shape[1:]
    planes = green_hat.shape[1]
    whole_x, whole_y = green_hat.shape[2:]
    site = block_site.reshape(1, slots)
    block = jax.ShapeDtypeStruct((wide * narrow, PX * planes, ROW), F32)
    masked, send = call(
        place_kernel,
        (jax.ShapeDtypeStruct((slots, 2 * cells), F32), block),
        (block_count, charges, projection, site, tables["spread"], *tables["forward_z"]),
        scalars=(0,),
        flops=10**9,
        moved=3 * 10**6,
    )
    recv = lax.all_to_all(send, ("wide", "narrow"), 0, 0, tiled=True)
    own = jnp.concatenate(
        [shifted(masked, "narrow", 1), masked, shifted(masked, "narrow", -1)], axis=0
    )
    before, after = shifted(own, "wide", 1), shifted(own, "wide", -1)
    near = call(
        near_kernel,
        jax.ShapeDtypeStruct((slots, 2 * cells), F32),
        (near_source, before, own, after, near_table),
        scratch=(
            pltpu.VMEM((9 * slots, 2 * cells), F32),
            pltpu.VMEM((slots, 2 * cells), F32),
        ),
        scalars=(0,),
        flops=10**10,
        moved=10**7,
    )
    lines = pltpu.VMEM((2 * whole_y // 128, whole_x // 2 * planes, 128), F32)
    send = call(
        functools.partial(plane_kernel, wide, narrow),
        block,
        (
            recv,
            green_hat,
            *tables["forward_y"],
            *tables["inverse_y"],
            tables["forward_x"],
            tables["inverse_x"],
        ),
        scratch=(lines, lines),
        flops=3 * 10**9,
        moved=9 * 10**6,
    )
    recv = lax.all_to_all(send, ("wide", "narrow"), 0, 0, tiled=True)
    return call(
        finish_kernel,
        jax.ShapeDtypeStruct((2, cells, slots), F32),
        (
            block_count,
            recv,
            projection,
            site,
            tables["gather"],
            *tables["inverse_z"],
            near,
        ),
        scalars=(0,),
        flops=10**9,
        moved=3 * 10**6,
    )


def solution(mesh):
    placed = (
        P(None, None, ("wide", "narrow")),
        P(),
        P(None, ("wide", "narrow"), None, None),
        P(),
        P(("wide", "narrow")),
        P(("wide", "narrow")),
        P(None, ("wide", "narrow")),
    )
    return jax.shard_map(
        per_device,
        mesh=mesh,
        in_specs=placed,
        out_specs=P(None, None, ("wide", "narrow")),
        check_vma=False,
    )
```

profile of v0, /device:TPU:1, one launch (start us, length us, event | category | flops | bytes accessed | tf_op | source)
XLA Modules:
  0.0 86.1 jit_solution(18316192471922529621)
XLA Ops:
  0.7 0.0 copy-start.1
  0.7 0.9 %copy-done.1 = f32[2,64,256]{2,1,0:T(8,128)S(1)} copy-done((f32[2,64,256]{2,1,0:T(8,128)S(1)}, f32[2,64,256]{2,1,0:T(8,128)}, u32[]{:S(2)}) %copy-start.1) | copy-done | bytes 131096
  1.6 0.0 copy-start.3
  1.6 0.8 copy-done.3
  2.3 0.0 copy-start.5
  2.3 0.7 copy-done.5
  3.0 0.0 copy-start.12
  3.0 1.0 %copy-done.12 = bf16[128,2048]{1,0:T(8,128)(2,1)S(1)} copy-done((bf16[128,2048]{1,0:T(8,128)(2,1)S(1)}, bf16[128,2048]{1,0:T(8,128)(2,1)}, u32[]{:S(2)}) %copy-start.12) | copy-done | bytes 524312
  4.0 0.0 copy-start.15
  4.0 0.9 %copy-done.15 = bf16[256,256]{1,0:T(8,128)(2,1)S(1)} copy-done((bf16[256,256]{1,0:T(8,128)(2,1)S(1)}, bf16[256,256]{1,0:T(8,128)(2,1)}, u32[]{:S(2)}) %copy-start.15) | copy-done | bytes 131096
  4.9 0.0 copy-start.16
  4.9 0.9 %copy-done.16 = bf16[256,256]{1,0:T(8,128)(2,1)S(1)} copy-done((bf16[256,256]{1,0:T(8,128)(2,1)S(1)}, bf16[256,256]{1,0:T(8,128)(2,1)}, u32[]{:S(2)}) %copy-start.16) | copy-done | bytes 131096
  5.8 0.0 copy-start.17
  5.8 0.0 copy-start.18
  5.9 2.3 %shard_map.181 = (f32[256,128]{1,0:T(8,128)S(1)}, f32[32,32,128]{2,1,0:T(8,128)}) custom-call(s32[1]{0:T(128)S(6)} %copy.22.count, f32[2,64,256]{2,1,0:T(8,128)S(1)} %copy-done.1, f32[64,64]{1,0:T(8,128)S(1)} %copy-done.3, s32[1,256]{1,0:T(1,128)S(1)} %bitcast.1, bf16[128,2048]{1,0:T(8,128)(2,1)S(1)} %copy-done.12, bf16[256,256]{1,0:T(8,128)(2,1)S(1)} %copy-done.16, ...), custom_call_target="tpu_custom_call" | custom-call | flops 1000000000 | bytes 3000000 | tf_op jit(solution)/shard_map/pallas_call | solution.py:251
  8.1 7.1 %all-to-all-start = ((f32[32,32,128]{2,1,0:T(8,128)}), f32[32,32,128]{2,1,0:T(8,128)S(1)}, u32[]{:S(2)}, u32[]{:S(2)}) async-start(f32[32,32,128]{2,1,0:T(8,128)} %get-tuple-element.7), calls=%async_computation | async-start | bytes 1048576 | tf_op jit(solution)/shard_map/all_to_all | solution.py:285
  15.2 3.3 %collective-permute-start = (f32[256,128]{1,0:T(8,128)S(1)}, f32[256,128]{1,0:T(8,128)S(1)}, u32[]{:S(2)}, u32[]{:S(2)}) collective-permute-start(f32[256,128]{1,0:T(8,128)S(1)} %get-tuple-element.8), channel_id=1, source_target_pairs={{0,1},{1,2},{2,3},{4,5},{5,6},{6,7},{8,9},{9,10},{10,11},{12,13},{... | collective-permute-start | bytes 393224 | tf_op jit(solution)/shard_map/ppermute | solution.py:265
  18.5 1.3 %collective-permute-start.1 = (f32[256,128]{1,0:T(8,128)S(1)}, f32[256,128]{1,0:T(8,128)S(1)}, u32[]{:S(2)}, u32[]{:S(2)}) collective-permute-start(f32[256,128]{1,0:T(8,128)S(1)} %get-tuple-element.8), channel_id=1, source_target_pairs={{1,0},{2,1},{3,2},{5,4},{6,5},{7,6},{9,8},{10,9},{11,10},{13,12},{... | collective-permute-start | bytes 393224 | tf_op jit(solution)/shard_map/ppermute | solution.py:265
  19.8 6.9 %collective-permute-done = f32[256,128]{1,0:T(8,128)S(1)} collective-permute-done((f32[256,128]{1,0:T(8,128)S(1)}, f32[256,128]{1,0:T(8,128)S(1)}, u32[]{:S(2)}, u32[]{:S(2)}) %collective-permute-start) | collective-permute-done | bytes 131104 | tf_op jit(solution)/shard_map/ppermute | solution.py:265
  26.8 0.1 collective-permute-done.1
  26.9 0.0 copy-start
  26.9 0.0 copy-start.2
  26.9 4.2 %collective-permute-start.3 = (f32[768,128]{1,0:T(8,128)S(1)}, f32[768,128]{1,0:T(8,128)S(1)}, u32[]{:S(2)}, u32[]{:S(2)}) collective-permute-start(f32[768,128]{1,0:T(8,128)S(1)} %constant_dynamic-update-slice_fusion.own), channel_id=1, source_target_pairs={{4,0},{8,4},{12,8},{16,12},{20,16},{24,20},{28,24},{5,1},{9,5},{13... | collective-permute-start | bytes 1179656 | tf_op jit(solution)/shard_map/ppermute | solution.py:265
  31.2 3.0 %collective-permute-start.2 = (f32[768,128]{1,0:T(8,128)S(1)}, f32[768,128]{1,0:T(8,128)}, u32[]{:S(2)}, u32[]{:S(2)}) collective-permute-start(f32[768,128]{1,0:T(8,128)S(1)} %constant_dynamic-update-slice_fusion.own), channel_id=1, source_target_pairs={{0,4},{4,8},{8,12},{12,16},{16,20},{20,24},{24,28},{1,5},{5,9},{9,... | collective-permute-start | bytes 1179656 | tf_op jit(solution)/shard_map/ppermute | solution.py:265
  34.2 0.0 all-to-all-done.recv
  34.2 0.0 copy-done.17
  34.2 0.0 copy-done.18
  34.2 0.0 copy-start.7
  34.2 1.2 %copy-done.7 = bf16[1024,512]{1,0:T(8,128)(2,1)S(1)} copy-done((bf16[1024,512]{1,0:T(8,128)(2,1)S(1)}, bf16[1024,512]{1,0:T(8,128)(2,1)}, u32[]{:S(2)}) %copy-start.7) | copy-done | bytes 1048600
  35.4 0.0 copy-start.8
  35.4 1.2 %copy-done.8 = bf16[1024,512]{1,0:T(8,128)(2,1)S(1)} copy-done((bf16[1024,512]{1,0:T(8,128)(2,1)S(1)}, bf16[1024,512]{1,0:T(8,128)(2,1)}, u32[]{:S(2)}) %copy-start.8) | copy-done | bytes 1048600
  36.6 0.0 copy-start.9
  36.6 1.2 %copy-done.9 = bf16[512,1024]{1,0:T(8,128)(2,1)S(1)} copy-done((bf16[512,1024]{1,0:T(8,128)(2,1)S(1)}, bf16[512,1024]{1,0:T(8,128)(2,1)}, u32[]{:S(2)}) %copy-start.9) | copy-done | bytes 1048600
  37.9 0.0 copy-start.10
  37.9 1.2 %copy-done.10 = bf16[512,1024]{1,0:T(8,128)(2,1)S(1)} copy-done((bf16[512,1024]{1,0:T(8,128)(2,1)S(1)}, bf16[512,1024]{1,0:T(8,128)(2,1)}, u32[]{:S(2)}) %copy-start.10) | copy-done | bytes 1048600
  39.1 6.5 %shard_map.182 = f32[32,32,128]{2,1,0:T(8,128)} custom-call(f32[32,32,128]{2,1,0:T(8,128)S(1)} %all-to-all-done.recv, f32[2,8,64,512]{3,2,1,0:T(8,128)} %green.1, bf16[512,1024]{1,0:T(8,128)(2,1)S(1)} %copy-done.10, bf16[512,1024]{1,0:T(8,128)(2,1)S(1)} %copy-done.9, bf16[1024,512]{1,0:T(8,128)(2,1)S(1)} %copy-done.8, bf16[1024,512]{1,0:T(8,128)(2,1)S(1)} %copy-done.7, ...), custom_call_target="tpu_custom_call" | custom-call | flops 3000000000 | bytes 9000000 | tf_op jit(solution)/shard_map/pallas_call | solution.py:251
  45.6 6.8 %all-to-all-start.1 = ((f32[32,32,128]{2,1,0:T(8,128)}), f32[32,32,128]{2,1,0:T(8,128)S(1)}, u32[]{:S(2)}, u32[]{:S(2)}) async-start(f32[32,32,128]{2,1,0:T(8,128)} %shard_map.182), calls=%async_computation.1 | async-start | bytes 1048576 | tf_op jit(solution)/shard_map/all_to_all | solution.py:318
  52.5 0.0 copy-start.4
  52.5 0.0 copy-start.6
  52.5 0.0 copy-start.13
  52.5 0.0 copy-start.14
  52.5 0.0 collective-permute-done.3.after
  52.5 0.0 collective-permute-done.2.before
  52.5 0.0 copy-done
  52.5 0.0 copy-done.2
  52.5 27.9 %shard_map.183.near = f32[256,128]{1,0:T(8,128)S(1)} custom-call(s32[27,256]{1,0:T(8,128)S(1)} %copy-done.2, f32[768,128]{1,0:T(8,128)} %collective-permute-done.2.before, f32[768,128]{1,0:T(8,128)S(1)} %constant_dynamic-update-slice_fusion.own, f32[768,128]{1,0:T(8,128)S(1)} %collective-permute-done.3.after, f32[27,2,64,64]{3,2,1,0:T(8,128)S(1)} %copy-done), custom_call_target="tpu_custom_call" | custom-call | flops 10000000000 | bytes 10000000 | tf_op jit(solution)/shard_map/pallas_call | solution.py:251
  80.5 0.0 copy-start.19
  80.5 0.6 copy-done.19
  81.1 0.0 all-to-all-done.1.recv
  81.1 0.0 copy-done.4
  81.1 0.0 copy-done.6
  81.1 0.0 copy-done.13
  81.1 0.0 copy-done.14
  81.2 0.0 copy-start.11
  81.2 1.0 %copy-done.11 = bf16[2048,128]{1,0:T(8,128)(2,1)S(1)} copy-done((bf16[2048,128]{1,0:T(8,128)(2,1)S(1)}, bf16[2048,128]{1,0:T(8,128)(2,1)}, u32[]{:S(2)}) %copy-start.11) | copy-done | bytes 524312
  82.2 0.0 copy-start.20
  82.2 0.9 %copy-done.20 = f32[256,128]{1,0:T(8,128)S(1)} copy-done((f32[256,128]{1,0:T(8,128)S(1)}, f32[256,128]{1,0:T(8,128)}, u32[]{:S(2)}) %copy-start.20) | copy-done | bytes 131096
  83.1 3.0 %shard_map.184 = f32[2,64,256]{2,1,0:T(8,128)} custom-call(s32[1]{0:T(128)S(6)} %copy.22.count, f32[32,32,128]{2,1,0:T(8,128)S(1)} %all-to-all-done.1.recv, f32[64,64]{1,0:T(8,128)S(1)} %copy-done.4, s32[1,256]{1,0:T(1,128)S(1)} %bitcast.2, bf16[2048,128]{1,0:T(8,128)(2,1)S(1)} %copy-done.11, bf16[128,512]{1,0:T(8,128)(2,1)S(1)} %copy-done.14, ...), custom_call_target="tpu_custom_call" | custom-call | flops 1000000000 | bytes 3000000 | tf_op jit(solution)/shard_map/pallas_call | solution.py:251
  (3 shorter events, 0.0 us)
Async XLA Ops:
  0.7 0.9 %copy-start.1 = (f32[2,64,256]{2,1,0:T(8,128)S(1)}, f32[2,64,256]{2,1,0:T(8,128)}, u32[]{:S(2)}) copy-start(f32[2,64,256]{2,1,0:T(8,128)} %charges.1) | copy-start | bytes 393220
  1.6 0.8 copy-start.3
  2.3 0.7 copy-start.5
  3.0 1.0 %copy-start.12 = (bf16[128,2048]{1,0:T(8,128)(2,1)S(1)}, bf16[128,2048]{1,0:T(8,128)(2,1)}, u32[]{:S(2)}) copy-start(bf16[128,2048]{1,0:T(8,128)(2,1)} %constant.24.clone.spread) | copy-start | bytes 1572868
  4.0 0.9 %copy-start.15 = (bf16[256,256]{1,0:T(8,128)(2,1)S(1)}, bf16[256,256]{1,0:T(8,128)(2,1)}, u32[]{:S(2)}) copy-start(bf16[256,256]{1,0:T(8,128)(2,1)} %constant.26.clone.zl) | copy-start | bytes 393220
  4.9 0.9 %copy-start.16 = (bf16[256,256]{1,0:T(8,128)(2,1)S(1)}, bf16[256,256]{1,0:T(8,128)(2,1)}, u32[]{:S(2)}) copy-start(bf16[256,256]{1,0:T(8,128)(2,1)} %constant.25.clone.zh) | copy-start | bytes 393220
  5.8 28.3 %copy-start.17 = (bf16[128,192]{1,0:T(8,128)(2,1)S(1)}, bf16[128,192]{1,0:T(8,128)(2,1)}, u32[]{:S(2)}) copy-start(bf16[128,192]{1,0:T(8,128)(2,1)} %constant.31.clone.fx) | copy-start | bytes 147460
  5.8 28.3 %copy-start.18 = (bf16[64,384]{1,0:T(8,128)(2,1)S(1)}, bf16[64,384]{1,0:T(8,128)(2,1)}, u32[]{:S(2)}) copy-start(bf16[64,384]{1,0:T(8,128)(2,1)} %constant.32.clone.ix) | copy-start | bytes 147460
  8.1 26.1 %all-to-all-start = ((f32[32,32,128]{2,1,0:T(8,128)}), f32[32,32,128]{2,1,0:T(8,128)S(1)}, u32[]{:S(2)}, u32[]{:S(2)}) async-start(f32[32,32,128]{2,1,0:T(8,128)} %get-tuple-element.7), calls=%async_computation | async-start | bytes 1048576 | tf_op jit(solution)/shard_map/all_to_all | solution.py:285
  15.2 11.5 %collective-permute-start = (f32[256,128]{1,0:T(8,128)S(1)}, f32[256,128]{1,0:T(8,128)S(1)}, u32[]{:S(2)}, u32[]{:S(2)}) collective-permute-start(f32[256,128]{1,0:T(8,128)S(1)} %get-tuple-element.8), channel_id=1, source_target_pairs={{0,1},{1,2},{2,3},{4,5},{5,6},{6,7},{8,9},{9,10},{10,11},{12,13},{... | collective-permute-start | bytes 393224 | tf_op jit(solution)/shard_map/ppermute | solution.py:265
  18.5 8.4 %collective-permute-start.1 = (f32[256,128]{1,0:T(8,128)S(1)}, f32[256,128]{1,0:T(8,128)S(1)}, u32[]{:S(2)}, u32[]{:S(2)}) collective-permute-start(f32[256,128]{1,0:T(8,128)S(1)} %get-tuple-element.8), channel_id=1, source_target_pairs={{1,0},{2,1},{3,2},{5,4},{6,5},{7,6},{9,8},{10,9},{11,10},{13,12},{... | collective-permute-start | bytes 393224 | tf_op jit(solution)/shard_map/ppermute | solution.py:265
  26.9 25.6 %copy-start = (f32[27,2,64,64]{3,2,1,0:T(8,128)S(1)}, f32[27,2,64,64]{3,2,1,0:T(8,128)}, u32[]{:S(2)}) copy-start(f32[27,2,64,64]{3,2,1,0:T(8,128)} %table.1) | copy-start | bytes 2654212
  26.9 25.6 %copy-start.2 = (s32[27,256]{1,0:T(8,128)S(1)}, s32[27,256]{1,0:T(8,128)}, u32[]{:S(2)}) copy-start(s32[27,256]{1,0:T(8,128)} %source.1) | copy-start | bytes 82948
  26.9 25.6 %collective-permute-start.3 = (f32[768,128]{1,0:T(8,128)S(1)}, f32[768,128]{1,0:T(8,128)S(1)}, u32[]{:S(2)}, u32[]{:S(2)}) collective-permute-start(f32[768,128]{1,0:T(8,128)S(1)} %constant_dynamic-update-slice_fusion.own), channel_id=1, source_target_pairs={{4,0},{8,4},{12,8},{16,12},{20,16},{24,20},{28,24},{5,1},{9,5},{13... | collective-permute-start | bytes 1179656 | tf_op jit(solution)/shard_map/ppermute | solution.py:265
  31.2 21.4 %collective-permute-start.2 = (f32[768,128]{1,0:T(8,128)S(1)}, f32[768,128]{1,0:T(8,128)}, u32[]{:S(2)}, u32[]{:S(2)}) collective-permute-start(f32[768,128]{1,0:T(8,128)S(1)} %constant_dynamic-update-slice_fusion.own), channel_id=1, source_target_pairs={{0,4},{4,8},{8,12},{12,16},{16,20},{20,24},{24,28},{1,5},{5,9},{9,... | collective-permute-start | bytes 1179656 | tf_op jit(solution)/shard_map/ppermute | solution.py:265
  34.2 1.2 %copy-start.7 = (bf16[1024,512]{1,0:T(8,128)(2,1)S(1)}, bf16[1024,512]{1,0:T(8,128)(2,1)}, u32[]{:S(2)}) copy-start(bf16[1024,512]{1,0:T(8,128)(2,1)} %constant.30.clone.iyl) | copy-start | bytes 3145732
  35.4 1.2 %copy-start.8 = (bf16[1024,512]{1,0:T(8,128)(2,1)S(1)}, bf16[1024,512]{1,0:T(8,128)(2,1)}, u32[]{:S(2)}) copy-start(bf16[1024,512]{1,0:T(8,128)(2,1)} %constant.29.clone.iyh) | copy-start | bytes 3145732
  36.6 1.2 %copy-start.9 = (bf16[512,1024]{1,0:T(8,128)(2,1)S(1)}, bf16[512,1024]{1,0:T(8,128)(2,1)}, u32[]{:S(2)}) copy-start(bf16[512,1024]{1,0:T(8,128)(2,1)} %constant.28.clone.fyl) | copy-start | bytes 3145732
  37.9 1.2 %copy-start.10 = (bf16[512,1024]{1,0:T(8,128)(2,1)S(1)}, bf16[512,1024]{1,0:T(8,128)(2,1)}, u32[]{:S(2)}) copy-start(bf16[512,1024]{1,0:T(8,128)(2,1)} %constant.27.clone.fyh) | copy-start | bytes 3145732
  45.6 35.5 %all-to-all-start.1 = ((f32[32,32,128]{2,1,0:T(8,128)}), f32[32,32,128]{2,1,0:T(8,128)S(1)}, u32[]{:S(2)}, u32[]{:S(2)}) async-start(f32[32,32,128]{2,1,0:T(8,128)} %shard_map.182), calls=%async_computation.1 | async-start | bytes 1048576 | tf_op jit(solution)/shard_map/all_to_all | solution.py:318
  52.5 28.7 %copy-start.4 = (f32[64,64]{1,0:T(8,128)S(1)}, f32[64,64]{1,0:T(8,128)}, u32[]{:S(2)}) copy-start(f32[64,64]{1,0:T(8,128)} %projection.3) | copy-start | bytes 49156
  52.5 28.7 %copy-start.6 = (s32[256]{0:T(256)S(1)}, s32[256]{0:T(256)}, u32[]{:S(2)}) copy-start(s32[256]{0:T(256)} %param.23) | copy-start | bytes 3076
  52.5 28.7 %copy-start.13 = (bf16[128,512]{1,0:T(8,128)(2,1)S(1)}, bf16[128,512]{1,0:T(8,128)(2,1)}, u32[]{:S(2)}) copy-start(bf16[128,512]{1,0:T(8,128)(2,1)} %constant.35.clone.zl) | copy-start | bytes 393220
  52.5 28.7 %copy-start.14 = (bf16[128,512]{1,0:T(8,128)(2,1)S(1)}, bf16[128,512]{1,0:T(8,128)(2,1)}, u32[]{:S(2)}) copy-start(bf16[128,512]{1,0:T(8,128)(2,1)} %constant.34.clone.zh) | copy-start | bytes 393220
  80.5 0.7 copy-start.19
  81.2 1.0 %copy-start.11 = (bf16[2048,128]{1,0:T(8,128)(2,1)S(1)}, bf16[2048,128]{1,0:T(8,128)(2,1)}, u32[]{:S(2)}) copy-start(bf16[2048,128]{1,0:T(8,128)(2,1)} %constant.33.clone.gather) | copy-start | bytes 1572868
  82.2 0.9 %copy-start.20 = (f32[256,128]{1,0:T(8,128)S(1)}, f32[256,128]{1,0:T(8,128)}, u32[]{:S(2)}) copy-start(f32[256,128]{1,0:T(8,128)} %copy-done.19) | copy-start | bytes 393220
where the time goes:
time: 87.1 us; the launch traced here: 86.1 us
  Pallas kernels  39.6 us (45%)
  starting transfers between devices  25.7 us (30%)
  local copies, waits for them, and re-layouts  12.7 us (15%)
  waiting for transfers between devices  7.05 us (8%)
  between operations  0.89 us (1%)
    pallas_call x4, Pallas kernels, call(): pl.pallas_call(kernel, out_shape=out_shape, in_specs=spaces, out_specs=ou...  39.6 us
    all_to_all x2, starting transfers between devices, per_device(): recv = lax.all_to_all(send, ('wide', 'narrow'), 0, 0, tiled=True)  13.9 us
    unnamed x44, local copies, waits for them, and re-layouts  12.7 us
    ppermute x4, starting transfers between devices, shifted(): return lax.ppermute(array, axis, pairs)  11.8 us
    ppermute x4, waiting for transfers between devices, shifted(): return lax.ppermute(array, axis, pairs)  7.05 us
  transfers between devices with their start and end apart: 6, of which 2 were waited for; matrix products, arithmetic and copies ran while one was open for 0% of the time, Pallas kernels for 40%

commit v1 on v0

v1 whole, which is shorter than its diff:
```python
import functools

import jax
import jax.numpy as jnp
import ml_dtypes
import numpy as np
from jax import lax
from jax.experimental import pallas as pl
from jax.experimental.pallas import tpu as pltpu
from jax.sharding import PartitionSpec as P

PX = 4
PY = 64
PZ = 128
SPAN_Y = PY // 4
SPAN_Z = PZ // 4
ROW = 2 * PY
WIDTH = PX * ROW
VMEM_LIMIT = 56 * 1024 * 1024
CLOSE = 9
F32 = jnp.float32
BF16 = jnp.bfloat16


def halves(table):
    high = table.astype(np.float32).astype(ml_dtypes.bfloat16)
    low = (table - high.astype(np.float64)).astype(np.float32).astype(ml_dtypes.bfloat16)
    return high, low


def waves(left, right, length):
    angles = 2.0 * np.pi * (np.outer(left, right) % length) / length
    return np.cos(angles), np.sin(angles)


@functools.lru_cache(maxsize=None)
def constant_tables(wide_count, narrow_count):
    whole_x = 2 * PX * wide_count
    whole_y = 2 * PY * narrow_count
    whole_z = 2 * PZ
    ez, ex, part, ey, _ = np.unravel_index(
        np.arange(4 * WIDTH), (4, PX, 2, 4, SPAN_Y)
    )
    owner = part * 64 + 16 * ex + 4 * ey + ez
    spread = (np.arange(128)[:, None] == owner[None, :]).astype(ml_dtypes.bfloat16)
    depth = (4 * np.arange(SPAN_Z)[None, :] + np.arange(4)[:, None]).reshape(-1)
    cos_z, sin_z = waves(np.arange(whole_z), depth, whole_z)
    forward_z = np.concatenate([cos_z, sin_z], axis=1)
    inverse_z = np.concatenate([cos_z.T, sin_z.T], axis=1) / (whole_x * whole_y * whole_z)
    line = (4 * np.arange(SPAN_Y)[None, :] + np.arange(4)[:, None]).reshape(-1)
    points = (PY * np.arange(narrow_count)[:, None] + line[None, :]).reshape(-1)
    cos_y, sin_y = waves(points, np.arange(whole_y), whole_y)
    real_rows = np.concatenate([cos_y, -sin_y], axis=1).reshape(narrow_count, 1, PY, 2 * whole_y)
    imag_rows = np.concatenate([sin_y, cos_y], axis=1).reshape(narrow_count, 1, PY, 2 * whole_y)
    forward_y = np.concatenate([real_rows, imag_rows], axis=1).reshape(-1, 2 * whole_y)
    cos_x, sin_x = waves(np.arange(whole_x), np.arange(whole_x // 2), whole_x)
    forward_x = np.block([[cos_x, sin_x], [-sin_x, cos_x]])
    packed = []
    for table in (forward_x, forward_x.T):
        high, low = halves(table)
        packed.append(np.concatenate([high, high, low], axis=1))
    return {
        "spread": spread,
        "gather": np.ascontiguousarray(spread.T),
        "forward_z": halves(forward_z),
        "inverse_z": halves(inverse_z),
        "forward_y": halves(forward_y),
        "inverse_y": halves(np.ascontiguousarray(forward_y.T)),
        "forward_x": packed[0],
        "inverse_x": packed[1],
    }


def split(values):
    high = values.astype(BF16)
    return high, (values - high.astype(F32)).astype(BF16)


def dot(left, right, dims=((1,), (0,))):
    return lax.dot_general(left, right, (dims, ((), ())), preferred_element_type=F32)


def dot3(left, right, dims=((1,), (0,))):
    lh, ll = left
    rh, rl = right
    return dot(lh, rh, dims) + (dot(ll, rh, dims) + dot(lh, rl, dims))


def turned(values, sign):
    lanes = lax.broadcasted_iota(jnp.int32, (values.shape[0], ROW), 1)
    factor = jnp.where(lanes < PY, sign, -sign).astype(F32)
    pieces = [
        pltpu.roll(values[:, i * ROW : (i + 1) * ROW], PY, 1) * factor
        for i in range(values.shape[1] // ROW)
    ]
    return jnp.concatenate(pieces, axis=1)


def columns_of(row, slots):
    return jnp.broadcast_to(row.astype(F32), (128, slots)).T


def own_line(site, slots):
    line = columns_of(site // SPAN_Z, slots)
    lanes = lax.broadcasted_iota(jnp.int32, (slots, 128), 1) % SPAN_Y
    match = line == lanes.astype(F32)
    return jnp.concatenate([match.astype(F32)] * (WIDTH // 128), axis=1)


def place(masked, projection, site, table):
    slots = masked.shape[1]
    cells = masked.shape[0] // 2
    weights = split(projection)
    stencil = jnp.concatenate(
        [dot3(weights, split(masked[r * cells : (r + 1) * cells])) for r in range(2)], axis=0
    ).T
    high, low = split(stencil)
    spread = dot(jnp.concatenate([high, low], axis=1), jnp.concatenate([table, table], axis=0))
    mask = own_line(site, slots)
    depth = lax.broadcasted_iota(jnp.int32, (SPAN_Z, slots), 0)
    picker = (depth == site % SPAN_Z).astype(F32).astype(BF16)
    rows = []
    for ez in range(4):
        high, low = split(spread[:, ez * WIDTH : (ez + 1) * WIDTH] * mask)
        rows.append(dot(picker, high) + dot(picker, low))
    grid = jnp.concatenate(rows, axis=0)
    return jnp.concatenate([grid, turned(grid, 1.0)], axis=0)


def gather_points(grid, site, slots, table):
    mask = own_line(site, slots)
    depth = lax.broadcasted_iota(jnp.int32, (slots, 128), 1)
    match = columns_of(site % SPAN_Z, slots) == depth.astype(F32)
    picker = match.astype(F32).astype(BF16)[:, :SPAN_Z]
    total = jnp.zeros((slots, 128), F32)
    for ez in range(4):
        high, low = split(grid[ez * SPAN_Z : (ez + 1) * SPAN_Z])
        taken = (dot(picker, high) + dot(picker, low)) * mask
        high, low = split(taken)
        rows = table[ez * WIDTH : (ez + 1) * WIDTH, :]
        total = total + (dot(high, rows) + dot(low, rows))
    return total.T


def plane_transforms(z, lines, back, green, fx, ix, planes):
    whole_x = green.shape[2]
    half_x = whole_x // 2
    chunks = lines.shape[0]
    at = pl.ds(z, half_x, stride=planes) if planes > 1 else pl.ds(0, half_x)
    taken = [lines[c, at, :] for c in range(chunks)]
    column = jnp.concatenate(
        [
            jnp.concatenate(taken[: chunks // 2], axis=1),
            jnp.concatenate(taken[chunks // 2 :], axis=1),
        ],
        axis=0,
    )
    high, low = split(column)
    freq = dot(fx[...], jnp.concatenate([high, low, high], axis=0))
    real, imag = freq[:whole_x], freq[whole_x:]
    gr, gi = green[0, z], green[1, z]
    product = jnp.concatenate([gr * real - gi * imag, gr * imag + gi * real], axis=0)
    high, low = split(product)
    column = dot(ix[...], jnp.concatenate([high, low, high], axis=0))
    for c in range(chunks):
        part, lane = divmod(c, chunks // 2)
        back[c, at, :] = column[
            part * half_x : (part + 1) * half_x, lane * 128 : (lane + 1) * 128
        ]


def near_class(k, source, table, close):
    slots = source.shape[1]
    row = source[pl.ds(k, 1), :]
    slot = lax.broadcasted_iota(jnp.int32, (slots, slots), 0)
    onehot = (slot == row % slots).astype(F32).astype(BF16)
    block = row // slots
    height = close.shape[0] // CLOSE
    picked = jnp.zeros((height, slots), F32)
    for i in range(CLOSE):
        some = dot(close[i * height : (i + 1) * height, :], onehot)
        picked = jnp.where(block == i, some, picked)
    picked = picked.astype(BF16)
    real, imag = table[k, 0], table[k, 1]
    matrix = jnp.concatenate(
        [jnp.concatenate([real, -imag], axis=1), jnp.concatenate([imag, real], axis=1)],
        axis=0,
    )
    high, low = split(matrix)
    return dot(jnp.concatenate([high, high], axis=1), picked) + dot(low, picked[: height // 2])


def operator_kernel(wide, narrow, loads, *refs):
    count, charges, projection, site, source = refs[:5]
    far_refs = refs[5 : 5 + loads]
    out = refs[5 + loads]
    held = refs[6 + loads : 6 + 2 * loads]
    (
        send_a, recv_a, send_b, recv_b, lines, back, cube, close, near,
        load_sem, send_sem_a, recv_sem_a, send_sem_b, recv_sem_b, halo_send, halo_recv,
    ) = refs[6 + 2 * loads :]
    spread, fzh, fzl, fyh, fyl, fx, green, ix, iyh, iyl, near_table, izh, izl, gather = held
    devices = wide * narrow
    w, n = lax.axis_index("wide"), lax.axis_index("narrow")
    me = w * narrow + n
    _, cells, slots = charges.shape
    planes = green.shape[1]
    chunks = lines.shape[0]
    group = PX * planes

    barrier = pltpu.get_barrier_semaphore()

    def place_of(step):
        to = lax.rem(me + step, devices)
        return to, (lax.div(to, narrow), lax.rem(to, narrow))

    def greet(step, carry):
        pl.semaphore_signal(
            barrier, inc=1, device_id=place_of(step)[1], device_id_type=pl.DeviceIdType.MESH
        )
        return carry

    lax.fori_loop(1, devices, greet, 0)
    copies = [
        pltpu.make_async_copy(far_refs[i], held[i], load_sem.at[i]) for i in range(loads)
    ]
    for copy in copies:
        copy.start()

    def exchange(step, send, recv, send_sem, recv_sem):
        to, device = place_of(step)
        return pltpu.make_async_remote_copy(
            src_ref=send.at[to],
            dst_ref=recv.at[me],
            send_sem=send_sem.at[step],
            recv_sem=recv_sem.at[step],
            device_id=device,
            device_id_type=pl.DeviceIdType.MESH,
        )

    def start_all(*buffers):
        def one(step, carry):
            exchange(step, *buffers).start()
            return carry

        lax.fori_loop(1, devices, one, 0)

    def receive_all(*buffers):
        def one(step, carry):
            exchange(step, *buffers).wait_recv()
            return carry

        lax.fori_loop(1, devices, one, 0)

    def sent_all(*buffers):
        def one(step, carry):
            exchange(step, *buffers).wait_send()
            return carry

        lax.fori_loop(1, devices, one, 0)

    def beside(index, src, dst, device):
        return pltpu.make_async_remote_copy(
            src_ref=src,
            dst_ref=dst,
            send_sem=halo_send.at[index],
            recv_sem=halo_recv.at[index],
            device_id=device,
            device_id_type=pl.DeviceIdType.MESH,
        )

    narrow_halo = (
        (n < narrow - 1, n > 0, beside(0, cube.at[4], cube.at[3], (w, n + 1))),
        (n > 0, n < narrow - 1, beside(1, cube.at[4], cube.at[5], (w, n - 1))),
    )
    wide_halo = (
        (w < wide - 1, w > 0, beside(2, cube.at[3:6], cube.at[0:3], (w + 1, n))),
        (w > 0, w < wide - 1, beside(3, cube.at[3:6], cube.at[6:9], (w - 1, n))),
    )

    def start_halo(halo):
        for sends, _, copy in halo:
            pl.when(sends)(copy.start)

    def receive_halo(halo):
        for _, receives, copy in halo:
            pl.when(receives)(copy.wait_recv)

    def sent_halo(halo):
        for sends, _, copy in halo:
            pl.when(sends)(copy.wait_send)

    for outside, blocks in (
        (n == 0, (3, 4)),
        (n == narrow - 1, (5, 6)),
        (w == 0, (0, 3)),
        (w == wide - 1, (6, 9)),
    ):

        @pl.when(outside)
        def _(blocks=blocks):
            for i in range(*blocks):
                cube[i] = jnp.zeros(cube.shape[1:], F32)

    slot = lax.broadcasted_iota(jnp.int32, (1, slots), 1)
    occupied = (slot < count[0]).astype(F32)
    masked = jnp.concatenate([charges[r] * occupied for r in range(2)], axis=0)
    cube[4] = masked
    copies[0].wait()
    grid = place(masked, projection[...], site[...], spread[...])
    copies[1].wait()
    copies[2].wait()
    freq = dot3((fzh[...], fzl[...]), split(grid))
    for ex in range(PX):
        block = freq[:, ex * ROW : (ex + 1) * ROW]
        send_a[:, ex * planes : (ex + 1) * planes, :] = block.reshape(devices, planes, ROW)

    pl.semaphore_wait(barrier, devices - 1)
    first = (send_a, recv_a, send_sem_a, recv_sem_a)
    start_all(*first)
    start_halo(narrow_halo)
    recv_a[pl.ds(me, 1)] = send_a[pl.ds(me, 1)]
    for copy in copies[3:]:
        copy.wait()
    receive_all(*first)

    values = recv_a[...].reshape(wide, narrow, group, ROW)
    field = jnp.concatenate(
        [values[:, i].reshape(wide * group, ROW) for i in range(narrow)], axis=1
    )
    freq = dot3(split(field), (fyh[...], fyl[...]))
    for c in range(chunks):
        lines[c] = freq[:, c * 128 : (c + 1) * 128]
    receive_halo(narrow_halo)
    start_halo(wide_halo)
    for z in range(planes):
        plane_transforms(z, lines, back, green, fx, ix, planes)
    field = jnp.concatenate([back[c] for c in range(chunks)], axis=1)
    result = dot3(split(field), (iyh[...], iyl[...]))
    for i in range(narrow):
        block = result[:, i * ROW : (i + 1) * ROW].reshape(wide, group, ROW)
        for j in range(wide):
            send_b[j * narrow + i] = block[j]
    second = (send_b, recv_b, send_sem_b, recv_sem_b)
    start_all(*second)
    recv_b[pl.ds(me, 1)] = send_b[pl.ds(me, 1)]

    receive_halo(wide_halo)
    rows = 2 * cells
    for i in range(CLOSE):
        high, low = split(cube[i])
        close[2 * i * rows : (2 * i + 1) * rows, :] = high
        close[(2 * i + 1) * rows : (2 * i + 2) * rows, :] = low
    near[...] = jnp.zeros(near.shape, F32)

    def one_class(k, carry):
        near[...] += near_class(k, source, near_table, close)
        return carry

    lax.fori_loop(0, source.shape[0], one_class, 0)

    receive_all(*second)
    freq = jnp.concatenate(
        [
            recv_b[:, ex * planes : (ex + 1) * planes, :].reshape(devices * planes, ROW)
            for ex in range(PX)
        ],
        axis=1,
    )
    both = jnp.concatenate([freq, turned(freq, -1.0)], axis=0)
    grid = dot3((izh[...], izl[...]), split(both))
    taken = gather_points(grid, site[...], slots, gather)
    weights = split(projection[...])
    for r in range(2):
        far = dot3(weights, split(taken[r * 64 : (r + 1) * 64]), ((0,), (0,)))
        out[r] = (far + near[r * cells : (r + 1) * cells, :]) * occupied
    sent_all(*first)
    sent_all(*second)
    sent_halo(narrow_halo)
    sent_halo(wide_halo)


def per_device(charges, projection, green_hat, near_table, block_site, block_count, near_source):
    wide = lax.axis_size("wide")
    narrow = lax.axis_size("narrow")
    devices = wide * narrow
    tables = constant_tables(wide, narrow)
    cells, slots = charges.shape[1:]
    planes = green_hat.shape[1]
    whole_x, whole_y = green_hat.shape[2:]
    loaded = (
        tables["spread"],
        *tables["forward_z"],
        *tables["forward_y"],
        tables["forward_x"],
        green_hat,
        tables["inverse_x"],
        *tables["inverse_y"],
        near_table,
        *tables["inverse_z"],
        tables["gather"],
    )
    block = pltpu.VMEM((devices, PX * planes, ROW), F32)
    lines = pltpu.VMEM((2 * whole_y // 128, whole_x // 2 * planes, 128), F32)
    one = pltpu.SemaphoreType.DMA((devices,))
    halo = pltpu.SemaphoreType.DMA((4,))
    vmem = pl.BlockSpec(memory_space=pltpu.VMEM)
    return pl.pallas_call(
        functools.partial(operator_kernel, wide, narrow, len(loaded)),
        out_shape=jax.ShapeDtypeStruct((2, cells, slots), F32),
        in_specs=[pl.BlockSpec(memory_space=pltpu.SMEM)]
        + [vmem] * 4
        + [pl.BlockSpec(memory_space=pl.ANY)] * len(loaded),
        out_specs=vmem,
        scratch_shapes=[pltpu.VMEM(array.shape, array.dtype) for array in loaded]
        + [block] * 4
        + [lines] * 2
        + [
            pltpu.VMEM((CLOSE, 2 * cells, slots), F32),
            pltpu.VMEM((CLOSE * 4 * cells, slots), BF16),
            pltpu.VMEM((2 * cells, slots), F32),
            pltpu.SemaphoreType.DMA((len(loaded),)),
        ]
        + [one] * 4
        + [halo] * 2,
        compiler_params=pltpu.CompilerParams(
            collective_id=0, has_side_effects=True, vmem_limit_bytes=VMEM_LIMIT
        ),
        cost_estimate=pl.CostEstimate(
            flops=2 * 10**10, bytes_accessed=2 * 10**7, transcendentals=0
        ),
    )(block_count, charges, projection, block_site.reshape(1, slots), near_source, *loaded)


def solution(mesh):
    placed = (
        P(None, None, ("wide", "narrow")),
        P(),
        P(None, ("wide", "narrow"), None, None),
        P(),
        P(("wide", "narrow")),
        P(("wide", "narrow")),
        P(None, ("wide", "narrow")),
    )
    return jax.shard_map(
        per_device,
        mesh=mesh,
        in_specs=placed,
        out_specs=P(None, None, ("wide", "narrow")),
        check_vma=False,
    )
```

time: 87.1 us -> 61.5 us (0.71)
  starting transfers between devices: 25.7 us -> 0 us
  Pallas kernels: 39.6 us -> 59.1 us
  local copies, waits for them, and re-layouts: 12.7 us -> 1.57 us
  waiting for transfers between devices: 7.05 us -> 0 us
    pallas_call x4 -> x1, Pallas kernels: 39.6 us -> 59.1 us  [per_device(): pl.pallas_call(functools.partial(operator_kernel, wide, narrow, len(loade...]
    all_to_all x2 -> x0, starting transfers between devices: 13.9 us -> none  [per_device(): recv = lax.all_to_all(send, ('wide', 'narrow'), 0, 0, tiled=True)]
    ppermute x4 -> x0, starting transfers between devices: 11.8 us -> none  [shifted(): return lax.ppermute(array, axis, pairs)]
    unnamed x44 -> x1, local copies, waits for them, and re-layouts: 12.7 us -> 1.57 us
    ppermute x4 -> x0, waiting for transfers between devices: 7.05 us -> none  [shifted(): return lax.ppermute(array, axis, pairs)]
  transfers between devices with their start and end apart: 6 -> 0, of which waited for: 2 -> 0; matrix products, arithmetic and copies ran while one was open for 0% -> 0% of each run, Pallas kernels for 40% -> 0%
where the time goes in v1:
time: 61.5 us; the launch traced here: 61.3 us
  Pallas kernels  59.1 us (96%)
  local copies, waits for them, and re-layouts  1.57 us (3%)
  between operations  0.66 us (1%)
    pallas_call x1, Pallas kernels, per_device(): pl.pallas_call(functools.partial(operator_kernel, wide, narrow, len(loade...  59.1 us
    unnamed x1, local copies, waits for them, and re-layouts  1.57 us

profile of v1, /device:TPU:1, one launch (start us, length us, event | category | flops | bytes accessed | tf_op | source)
XLA Modules:
  0.0 61.3 jit_solution(8641907087332839251)
XLA Ops:
  0.7 59.1 %shard_map.181 = f32[2,64,256]{2,1,0:T(8,128)} custom-call(s32[1]{0:T(128)S(6)} %copy.21.refs_0_, f32[2,64,256]{2,1,0:T(8,128)} %refs_1_.1, f32[64,64]{1,0:T(8,128)} %refs_2_.1, s32[1,256]{1,0:T(1,128)} %bitcast.1, s32[27,256]{1,0:T(8,128)} %refs_4_.1, bf16[128,2048]{1,0:T(8,128)(2,1)} %constant.24.clone.refs_5_, bf16[256,256]{1,0:T(8,128)(2,1)} %constant.25.clone.refs_6_, ...), custom_call_target="tpu_custom_call" | custom-call | flops 20000000000 | bytes 20000000 | tf_op jit(solution)/shard_map/pallas_call | solution.py:408
  59.7 1.6 %copy.22 = f32[2,64,256]{2,1,0:T(8,128)} copy(f32[2,64,256]{2,1,0:T(8,128)} %shard_map.181) | data formatting | bytes 262144

commit v2 on v1

--- a/solution.py
+++ b/solution.py
@@ -33,6 +33,10 @@
     return np.cos(angles), np.sin(angles)
 
 
+def parts_of(planes):
+    return 2 if planes % 8 == 0 else 1
+
+
 @functools.lru_cache(maxsize=None)
 def constant_tables(wide_count, narrow_count):
     whole_x = 2 * PX * wide_count
@@ -44,7 +48,12 @@
     owner = part * 64 + 16 * ex + 4 * ey + ez
     spread = (np.arange(128)[:, None] == owner[None, :]).astype(ml_dtypes.bfloat16)
     depth = (4 * np.arange(SPAN_Z)[None, :] + np.arange(4)[:, None]).reshape(-1)
-    cos_z, sin_z = waves(np.arange(whole_z), depth, whole_z)
+    devices = wide_count * narrow_count
+    planes = whole_z // devices
+    parts = parts_of(planes)
+    order = np.arange(whole_z).reshape(devices, parts, planes // parts)
+    order = order.transpose(1, 0, 2).reshape(-1)
+    cos_z, sin_z = waves(order, depth, whole_z)
     forward_z = np.concatenate([cos_z, sin_z], axis=1)
     inverse_z = np.concatenate([cos_z.T, sin_z.T], axis=1) / (whole_x * whole_y * whole_z)
     line = (4 * np.arange(SPAN_Y)[None, :] + np.arange(4)[:, None]).reshape(-1)
@@ -53,7 +62,8 @@
     real_rows = np.concatenate([cos_y, -sin_y], axis=1).reshape(narrow_count, 1, PY, 2 * whole_y)
     imag_rows = np.concatenate([sin_y, cos_y], axis=1).reshape(narrow_count, 1, PY, 2 * whole_y)
     forward_y = np.concatenate([real_rows, imag_rows], axis=1).reshape(-1, 2 * whole_y)
-    cos_x, sin_x = waves(np.arange(whole_x), np.arange(whole_x // 2), whole_x)
+    near_x = (PX * np.arange(wide_count)[None, :] + np.arange(PX)[:, None]).reshape(-1)
+    cos_x, sin_x = waves(np.arange(whole_x), near_x, whole_x)
     forward_x = np.block([[cos_x, sin_x], [-sin_x, cos_x]])
     packed = []
     for table in (forward_x, forward_x.T):
@@ -142,12 +152,14 @@
     return total.T
 
 
-def plane_transforms(z, lines, back, green, fx, ix, planes):
-    whole_x = green.shape[2]
+def plane_transforms(z, lines, back, green, fx, ix, wide, group):
+    whole_x = green.shape[1]
     half_x = whole_x // 2
     chunks = lines.shape[0]
-    at = pl.ds(z, half_x, stride=planes) if planes > 1 else pl.ds(0, half_x)
-    taken = [lines[c, at, :] for c in range(chunks)]
+    rows = [pl.ds(z * PX + ex, wide, stride=group) for ex in range(PX)]
+    taken = [
+        jnp.concatenate([lines[c, at, :] for at in rows], axis=0) for c in range(chunks)
+    ]
     column = jnp.concatenate(
         [
             jnp.concatenate(taken[: chunks // 2], axis=1),
@@ -158,36 +170,42 @@
     high, low = split(column)
     freq = dot(fx[...], jnp.concatenate([high, low, high], axis=0))
     real, imag = freq[:whole_x], freq[whole_x:]
-    gr, gi = green[0, z], green[1, z]
+    gr, gi = green[0], green[1]
     product = jnp.concatenate([gr * real - gi * imag, gr * imag + gi * real], axis=0)
     high, low = split(product)
     column = dot(ix[...], jnp.concatenate([high, low, high], axis=0))
     for c in range(chunks):
         part, lane = divmod(c, chunks // 2)
-        back[c, at, :] = column[
-            part * half_x : (part + 1) * half_x, lane * 128 : (lane + 1) * 128
-        ]
-
-
-def near_class(k, source, table, close):
+        for ex, at in enumerate(rows):
+            top = part * half_x + ex * wide
+            back[c, at, :] = column[top : top + wide, lane * 128 : (lane + 1) * 128]
+
+
+def near_prepare(k, source, table, close, onehots, matrices, picked):
     slots = source.shape[1]
     row = source[pl.ds(k, 1), :]
     slot = lax.broadcasted_iota(jnp.int32, (slots, slots), 0)
     onehot = (slot == row % slots).astype(F32).astype(BF16)
-    block = row // slots
-    height = close.shape[0] // CLOSE
-    picked = jnp.zeros((height, slots), F32)
-    for i in range(CLOSE):
-        some = dot(close[i * height : (i + 1) * height, :], onehot)
-        picked = jnp.where(block == i, some, picked)
-    picked = picked.astype(BF16)
+    onehots[k] = onehot
     real, imag = table[k, 0], table[k, 1]
     matrix = jnp.concatenate(
         [jnp.concatenate([real, -imag], axis=1), jnp.concatenate([imag, real], axis=1)],
         axis=0,
     )
     high, low = split(matrix)
-    return dot(jnp.concatenate([high, high], axis=1), picked) + dot(low, picked[: height // 2])
+    matrices[k] = jnp.concatenate([high, high, low], axis=1)
+    some = dot(close[CLOSE // 2], onehot)
+    picked[k] = jnp.where(row // slots == CLOSE // 2, some, 0.0).astype(BF16)
+
+
+def near_pick(k, blocks, source, close, onehots, picked):
+    slots = source.shape[1]
+    block = source[pl.ds(k, 1), :] // slots
+    onehot = onehots[k]
+    columns = picked[k].astype(F32)
+    for i in blocks:
+        columns = jnp.where(block == i, dot(close[i], onehot), columns)
+    return columns.astype(BF16)
 
 
 def operator_kernel(wide, narrow, loads, *refs):
@@ -196,7 +214,7 @@
     out = refs[5 + loads]
     held = refs[6 + loads : 6 + 2 * loads]
     (
-        send_a, recv_a, send_b, recv_b, lines, back, cube, close, near,
+        send_a, recv_a, send_b, recv_b, lines, back, cube, close, near, onehots, matrices, picked,
         load_sem, send_sem_a, recv_sem_a, send_sem_b, recv_sem_b, halo_send, halo_recv,
     ) = refs[6 + 2 * loads :]
     spread, fzh, fzl, fyh, fyl, fx, green, ix, iyh, iyl, near_table, izh, izl, gather = held
@@ -206,7 +224,14 @@
     _, cells, slots = charges.shape
     planes = green.shape[1]
     chunks = lines.shape[0]
-    group = PX * planes
+    parts = parts_of(planes)
+    part_planes = planes // parts
+    group = send_a.shape[1] // devices
+    spacing = group // part_planes
+    classes = source.shape[0]
+    if group > PX * part_planes:
+        send_a[...] = jnp.zeros(send_a.shape, F32)
+        back[...] = jnp.zeros(back.shape, F32)
 
     barrier = pltpu.get_barrier_semaphore()
 
@@ -227,13 +252,16 @@
     for copy in copies:
         copy.start()
 
-    def exchange(step, send, recv, send_sem, recv_sem):
+    def rows_of(device):
+        return pl.ds(pl.multiple_of(device * group, 8), group)
+
+    def exchange(step, part, send, recv, send_sem, recv_sem):
         to, device = place_of(step)
         return pltpu.make_async_remote_copy(
-            src_ref=send.at[to],
-            dst_ref=recv.at[me],
-            send_sem=send_sem.at[step],
-            recv_sem=recv_sem.at[step],
+            src_ref=send.at[part, rows_of(to)],
+            dst_ref=recv.at[part, rows_of(me)],
+            send_sem=send_sem.at[part, step],
+            recv_sem=recv_sem.at[part, step],
             device_id=device,
             device_id_type=pl.DeviceIdType.MESH,
         )
@@ -311,58 +339,101 @@
     copies[1].wait()
     copies[2].wait()
     freq = dot3((fzh[...], fzl[...]), split(grid))
-    for ex in range(PX):
-        block = freq[:, ex * ROW : (ex + 1) * ROW]
-        send_a[:, ex * planes : (ex + 1) * planes, :] = block.reshape(devices, planes, ROW)
-
+    some = devices * part_planes
+    for p in range(parts):
+        for ex in range(PX):
+            send_a[p, pl.ds(ex, some, stride=spacing), :] = freq[
+                p * some : (p + 1) * some, ex * ROW : (ex + 1) * ROW
+            ]
+
+    first = (send_a, recv_a, send_sem_a, recv_sem_a)
+    second = (send_b, recv_b, send_sem_b, recv_sem_b)
     pl.semaphore_wait(barrier, devices - 1)
-    first = (send_a, recv_a, send_sem_a, recv_sem_a)
-    start_all(*first)
+    start_all(0, *first)
     start_halo(narrow_halo)
-    recv_a[pl.ds(me, 1)] = send_a[pl.ds(me, 1)]
+    for p in range(1, parts):
+        start_all(p, *first)
+    for p in range(parts):
+        recv_a[p, rows_of(me), :] = send_a[p, rows_of(me), :]
+
+    def own_copy(i):
+        high, low = split(cube[i])
+        close[i] = jnp.concatenate([high, low], axis=0)
+
+    def each_class(body):
+        def three(j, carry):
+            for u in range(3):
+                body(3 * j + u)
+            return carry
+
+        lax.fori_loop(0, classes // 3, three, 0)
+        for k in range(classes - classes % 3, classes):
+            body(k)
+
+    own_copy(4)
+    near[...] = jnp.zeros(near.shape, F32)
     for copy in copies[3:]:
         copy.wait()
-    receive_all(*first)
-
-    values = recv_a[...].reshape(wide, narrow, group, ROW)
-    field = jnp.concatenate(
-        [values[:, i].reshape(wide * group, ROW) for i in range(narrow)], axis=1
-    )
-    freq = dot3(split(field), (fyh[...], fyl[...]))
-    for c in range(chunks):
-        lines[c] = freq[:, c * 128 : (c + 1) * 128]
-    receive_halo(narrow_halo)
-    start_halo(wide_halo)
-    for z in range(planes):
-        plane_transforms(z, lines, back, green, fx, ix, planes)
-    field = jnp.concatenate([back[c] for c in range(chunks)], axis=1)
-    result = dot3(split(field), (iyh[...], iyl[...]))
-    for i in range(narrow):
-        block = result[:, i * ROW : (i + 1) * ROW].reshape(wide, group, ROW)
-        for j in range(wide):
-            send_b[j * narrow + i] = block[j]
-    second = (send_b, recv_b, send_sem_b, recv_sem_b)
-    start_all(*second)
-    recv_b[pl.ds(me, 1)] = send_b[pl.ds(me, 1)]
+    each_class(
+        lambda k: near_prepare(k, source, near_table, close, onehots, matrices, picked)
+    )
+
+    def part_transforms(p):
+        values = recv_a[p].reshape(wide, narrow, group, ROW)
+        field = jnp.concatenate(
+            [values[:, i].reshape(wide * group, ROW) for i in range(narrow)], axis=1
+        )
+        freq = dot3(split(field), (fyh[...], fyl[...]))
+        for c in range(chunks):
+            lines[c] = freq[:, c * 128 : (c + 1) * 128]
+        for z in range(part_planes):
+            plane_transforms(
+                z, lines, back, green[:, p * part_planes + z], fx, ix, wide, group
+            )
+        field = jnp.concatenate([back[c] for c in range(chunks)], axis=1)
+        result = dot3(split(field), (iyh[...], iyl[...]))
+        for i in range(narrow):
+            for j in range(wide):
+                top = (j * narrow + i) * group
+                send_b[p, top : top + group, :] = result[
+                    j * group : (j + 1) * group, i * ROW : (i + 1) * ROW
+                ]
+        start_all(p, *second)
+        recv_b[p, rows_of(me), :] = send_b[p, rows_of(me), :]
+
+    for p in range(parts):
+        receive_all(p, *first)
+        part_transforms(p)
+        if p == 0:
+            receive_halo(narrow_halo)
+            start_halo(wide_halo)
+            own_copy(3)
+            own_copy(5)
+
+            def narrow_class(k):
+                picked[k] = near_pick(k, (3, 5), source, close, onehots, picked)
+
+            each_class(narrow_class)
 
     receive_halo(wide_halo)
-    rows = 2 * cells
-    for i in range(CLOSE):
-        high, low = split(cube[i])
-        close[2 * i * rows : (2 * i + 1) * rows, :] = high
-        close[(2 * i + 1) * rows : (2 * i + 2) * rows, :] = low
-    near[...] = jnp.zeros(near.shape, F32)
-
-    def one_class(k, carry):
-        near[...] += near_class(k, source, near_table, close)
-        return carry
-
-    lax.fori_loop(0, source.shape[0], one_class, 0)
-
-    receive_all(*second)
+    others = (0, 1, 2, 6, 7, 8)
+    for i in others:
+        own_copy(i)
+
+    def wide_class(k):
+        columns = near_pick(k, others, source, close, onehots, picked)
+        columns = jnp.concatenate([columns, columns[: 2 * cells]], axis=0)
+        near[...] += dot(matrices[k], columns)
+
+    each_class(wide_class)
+
+    for p in range(parts):
+        receive_all(p, *second)
     freq = jnp.concatenate(
         [
-            recv_b[:, ex * planes : (ex + 1) * planes, :].reshape(devices * planes, ROW)
+            jnp.concatenate(
+                [recv_b[p, pl.ds(ex, some, stride=spacing), :] for p in range(parts)], axis=0
+            )
             for ex in range(PX)
         ],
         axis=1,
@@ -374,8 +445,9 @@
     for r in range(2):
         far = dot3(weights, split(taken[r * 64 : (r + 1) * 64]), ((0,), (0,)))
         out[r] = (far + near[r * cells : (r + 1) * cells, :]) * occupied
-    sent_all(*first)
-    sent_all(*second)
+    for p in range(parts):
+        sent_all(p, *first)
+        sent_all(p, *second)
     sent_halo(narrow_halo)
     sent_halo(wide_halo)
 
@@ -400,9 +472,12 @@
         *tables["inverse_z"],
         tables["gather"],
     )
-    block = pltpu.VMEM((devices, PX * planes, ROW), F32)
-    lines = pltpu.VMEM((2 * whole_y // 128, whole_x // 2 * planes, 128), F32)
-    one = pltpu.SemaphoreType.DMA((devices,))
+    parts = parts_of(planes)
+    group = max(8, PX * planes // parts)
+    classes = near_source.shape[0]
+    block = pltpu.VMEM((parts, devices * group, ROW), F32)
+    lines = pltpu.VMEM((2 * whole_y // 128, wide * group, 128), F32)
+    one = pltpu.SemaphoreType.DMA((parts, devices))
     halo = pltpu.SemaphoreType.DMA((4,))
     vmem = pl.BlockSpec(memory_space=pltpu.VMEM)
     return pl.pallas_call(
@@ -417,8 +492,11 @@
         + [lines] * 2
         + [
             pltpu.VMEM((CLOSE, 2 * cells, slots), F32),
-            pltpu.VMEM((CLOSE * 4 * cells, slots), BF16),
+            pltpu.VMEM((CLOSE, 4 * cells, slots), BF16),
             pltpu.VMEM((2 * cells, slots), F32),
+            pltpu.VMEM((classes, slots, slots), BF16),
+            pltpu.VMEM((classes, 2 * cells, 6 * cells), BF16),
+            pltpu.VMEM((classes, 4 * cells, slots), BF16),
             pltpu.SemaphoreType.DMA((len(loaded),)),
         ]
         + [one] * 4

time: 61.5 us -> 53.7 us (0.87)
  Pallas kernels: 59.1 us -> 51.3 us
    pallas_call x1, Pallas kernels: 59.1 us -> 51.3 us  [per_device(): pl.pallas_call(functools.partial(operator_kernel, wide, narrow, len(loade...]
where the time goes in v2:
time: 53.7 us; the launch traced here: 53.6 us
  Pallas kernels  51.3 us (96%)
  local copies, waits for them, and re-layouts  1.57 us (3%)
  between operations  0.66 us (1%)
    pallas_call x1, Pallas kernels, per_device(): pl.pallas_call(functools.partial(operator_kernel, wide, narrow, len(loade...  51.3 us
    unnamed x1, local copies, waits for them, and re-layouts  1.57 us

profile of v2, /device:TPU:1, one launch (start us, length us, event | category | flops | bytes accessed | tf_op | source)
XLA Modules:
  0.0 53.6 jit_solution(6227550874609328509)
XLA Ops:
  0.7 51.3 %shard_map.181 = f32[2,64,256]{2,1,0:T(8,128)} custom-call(s32[1]{0:T(128)S(6)} %copy.21.refs_0_, f32[2,64,256]{2,1,0:T(8,128)} %refs_1_.1, f32[64,64]{1,0:T(8,128)} %refs_2_.1, s32[1,256]{1,0:T(1,128)} %bitcast.1, s32[27,256]{1,0:T(8,128)} %refs_4_.1, bf16[128,2048]{1,0:T(8,128)(2,1)} %constant.24.clone.refs_5_, bf16[256,256]{1,0:T(8,128)(2,1)} %constant.25.clone.refs_6_, ...), custom_call_target="tpu_custom_call" | custom-call | flops 20000000000 | bytes 20000000 | tf_op jit(solution)/shard_map/pallas_call | solution.py:483
  52.0 1.6 %copy.22 = f32[2,64,256]{2,1,0:T(8,128)} copy(f32[2,64,256]{2,1,0:T(8,128)} %shard_map.181) | data formatting | bytes 262144
